TPU v7x, 32 devices: a whole 2x2x4 slice. The times are simulated.
32 devices in a mesh: recon: 2 (over y), space: 4 (over z), grp: 4 (over x, core).
Axes of the slice: x: 2, y: 2, z: 4, core: 2. Of those that a mesh axis runs over, the one named last changes fastest.
Arguments:
- warm_sources: float32 [16, 16, 128, 256], P(('recon', 'grp'), 'space'), parts along dimension 0, may hold values from -16 to 16
- warm_detectors: float32 [16, 16, 128, 256], P(('recon', 'grp'), 'space'), parts along dimension 0, may hold values from -16 to 16
- source_positions: int32 [16], P(('recon', 'grp')), parts along dimension 0, may hold values from 0 to 4095
- detector_positions: int32 [16], P(('recon', 'grp')), parts along dimension 0, may hold values from 0 to 4095
- labels: int32 [32, 128, 256], P(('recon', 'space')), parts along dimension 0, may hold values from 0 to 7
- absorption: float32 [8], replicated, may hold values from 0.02 to 0.6
- residual_codes: int32 [16, 8], P('recon'), parts along dimension 0, may hold values from -64 to 63
Outputs:
- source_fields: float32 [16, 16, 128, 256], P(('recon', 'grp'), 'space'), parts along dimension 0
- detector_fields: float32 [16, 16, 128, 256], P(('recon', 'grp'), 'space'), parts along dimension 0
- gradient: float32 [32, 128, 256], P(('recon', 'space'), 'grp'), parts along dimension 0
There are 2 independent parts, one for each index of `recon`. A program takes and returns all parts, laid end to end along the dimension named above; an argument that names none is the same for every part. Nothing has to cross between parts.
All inputs are finite; a program needn't handle non-finite values.
Results may differ from a plain program's by a relative error of at most 0.0055.
Values may be sent and summed in bfloat16 or wider, within the bound.
A program may use at most 64 MiB of HBM per device.

v0:
```python
import jax
import jax.numpy as jnp
from jax import lax
from jax.sharding import PartitionSpec as P

ITERS = 2


source_power = 50.0
code_scale = 1.0 / 1024.0


def with_halo(array, sides, width):
    for axis, dim in sides:
        devices, length = (lax.axis_size(axis), array.shape[dim])
        up = [(i, (i + 1) % devices) for i in range(devices - 1)]
        down = [(j, i) for i, j in up]
        last = lax.slice_in_dim(array, length - width, length, axis=dim)
        initial = lax.slice_in_dim(array, 0, width, axis=dim)
        before = lax.ppermute(last, axis, up)
        after = lax.ppermute(initial, axis, down)
        array = jnp.concatenate([before, array, after], axis=dim)
    return array


def operate(field, diagonal):
    padded = with_halo(field, (("space", 1),), 1)
    beside = padded[:, 2:] + padded[:, :-2]
    flat_pad = jnp.pad(field, ((0, 0), (0, 0), (1, 1), (1, 1)))
    beside = beside + flat_pad[:, :, 2:, 1:-1] + flat_pad[:, :, :-2, 1:-1]
    beside = beside + flat_pad[:, :, 1:-1, 2:] + flat_pad[:, :, 1:-1, :-2]
    return diagonal[None] * field - beside


def point_drive(positions, x_face, first_plane, planes, breadth, extent):
    plane_at = positions // extent - first_plane
    column_at = positions % extent
    plane_ids = jnp.arange(planes, dtype=jnp.int32)
    column_ids = jnp.arange(extent, dtype=jnp.int32)
    face = (plane_ids[None, :, None] == plane_at[:, None, None]) & (
        column_ids[None, None, :] == column_at[:, None, None]
    )
    face_values = jnp.where(face, jnp.float32(source_power), jnp.float32(0.0))
    row_ids = jnp.arange(breadth, dtype=jnp.int32)
    return jnp.where(
        row_ids[None, None, :, None] == x_face, face_values[:, :, None, :], jnp.float32(0.0)
    )


def column(values):
    return values[:, None, None, None]


def inner_sums(first, second):
    return lax.psum(jnp.sum(first * second, axis=(1, 2, 3)), "space")


def local(
    warm_sources,
    warm_detectors,
    source_positions,
    detector_positions,
    labels,
    absorption,
    residual_codes,
):
    src_count = warm_sources.shape[0]
    det_count = warm_detectors.shape[0]
    planes, breadth, extent = labels.shape
    diagonal = jnp.full(labels.shape, 6.0, jnp.float32)
    for region in range(absorption.shape[0]):
        diagonal = diagonal + jnp.where(labels == region, absorption[region], jnp.float32(0.0))
    first_plane = lax.axis_index("space") * planes
    drive = jnp.concatenate(
        [
            point_drive(source_positions, 0, first_plane, planes, breadth, extent),
            point_drive(detector_positions, breadth - 1, first_plane, planes, breadth, extent),
        ],
        axis=0,
    )
    fields = jnp.concatenate([warm_sources, warm_detectors], axis=0)
    residual = drive - operate(fields, diagonal)
    direction = residual
    norm_now = inner_sums(residual, residual)
    for sweep in range(ITERS):
        image = operate(direction, diagonal)
        alpha = norm_now / inner_sums(direction, image)
        fields = fields + column(alpha) * direction
        residual = residual - column(alpha) * image
        if sweep + 1 < ITERS:
            norm_next = inner_sums(residual, residual)
            direction = residual + column(norm_next / norm_now) * direction
            norm_now = norm_next
    source_fields = fields[:src_count]
    detector_fields = fields[src_count:]
    weights_all = (residual_codes.astype(jnp.float32) * code_scale).astype(jnp.bfloat16)
    packed = fields.astype(jnp.bfloat16)
    block = lax.all_to_all(packed, "grp", split_axis=2, concat_axis=0, tiled=True)
    item_count = block.shape[1]
    groups = block.shape[0] // (src_count + det_count)
    grouped = block.reshape(groups, src_count + det_count, -1)
    source_flat = grouped[:, :src_count].reshape(groups * src_count, -1)
    detector_flat = grouped[:, src_count:].reshape(groups * det_count, -1)
    mixed = jnp.dot(weights_all, detector_flat, preferred_element_type=jnp.float32)
    owned = -jnp.sum(source_flat.astype(jnp.float32) * mixed, axis=0)
    gradient = owned.reshape(item_count, block.shape[2], block.shape[3])
    return (source_fields, detector_fields, gradient)


def solution(mesh):
    placed = (
        P(("recon", "grp"), "space", None, None),
        P(("recon", "grp"), "space", None, None),
        P(("recon", "grp")),
        P(("recon", "grp")),
        P(("recon", "space"), None, None),
        P(),
        P("recon", None),
    )
    return jax.shard_map(
        local,
        mesh=mesh,
        in_specs=placed,
        out_specs=(
            P(("recon", "grp"), "space", None, None),
            P(("recon", "grp"), "space", None, None),
            P(("recon", "space"), "grp", None),
        ),
        check_vma=False,
    )
```

profile of v0, /device:TPU:1, one launch (start us, length us, event | category | flops | bytes accessed | tf_op | source)
XLA Modules:
  0.0 123.0 jit_solution(3541429600715337499)
XLA Ops:
  0.6 1.4 %constant_dynamic-update-slice_fusion.1 = f32[4,4,128,256]{3,2,1,0:T(8,128)S(1)} fusion(f32[2,4,128,256]{3,2,1,0:T(8,128)} %param.7), kind=kLoop, calls=%fused_computation.54 | loop fusion | bytes 2097152
  2.0 0.1 copy-done.3
  2.3 1.3 %copy-done = f32[4,4,128,256]{3,2,1,0:T(8,128)} copy-done((f32[4,4,128,256]{3,2,1,0:T(8,128)}, f32[4,4,128,256]{3,2,1,0:T(8,128)S(1)}, u32[]{:S(2)}) %copy-start) | copy-done | bytes 2097176
  3.6 0.1 fusion.31
  3.7 1.3 %collective-permute-start = (f32[4,1,128,256]{3,2,1,0:T(8,128)S(1)}, f32[4,1,128,256]{3,2,1,0:T(8,128)S(1)}, u32[]{:S(2)}, u32[]{:S(2)}) collective-permute-start(f32[4,1,128,256]{3,2,1,0:T(8,128)S(1)} %get-tuple-element.19), channel_id=1, source_target_pairs={{4,0},{8,4},{12,8},{5,1},{9,5},{13,9},{6,2},{10,6},{14,10},{7,3},{... | collective-permute-start | bytes 1572872 | tf_op jit(solution)/shard_map/ppermute | solution.py:21
  5.0 5.5 %collective-permute-start.1 = (f32[4,1,128,256]{3,2,1,0:T(8,128)S(1)}, f32[4,1,128,256]{3,2,1,0:T(8,128)}, u32[]{:S(2)}, u32[]{:S(2)}) collective-permute-start(f32[4,1,128,256]{3,2,1,0:T(8,128)S(1)} %get-tuple-element.20), channel_id=1, source_target_pairs={{0,4},{4,8},{8,12},{1,5},{5,9},{9,13},{2,6},{6,10},{10,14},{3,7},{... | collective-permute-start | bytes 1572872 | tf_op jit(solution)/shard_map/ppermute | solution.py:20
  10.5 0.1 iota_compare_fusion.3
  10.6 0.1 iota_compare_fusion.2
  10.7 0.1 iota_compare_fusion.1
  10.7 0.1 iota_compare_fusion
  10.8 0.7 fusion.33
  11.5 0.1 and_select_fusion
  11.6 0.1 and_select_fusion.1
  11.6 5.7 %select_add_fusion = f32[4,128,256]{2,1,0:T(8,128)S(1)} fusion(s32[4,128,256]{2,1,0:T(8,128)S(1)} %copy-done.4, f32[]{:T(128)} %bitcast.7, f32[]{:T(128)} %bitcast.6, f32[]{:T(128)} %bitcast.5, f32[]{:T(128)} %bitcast.4, f32[]{:T(128)} %bitcast.3, f32[]{:T(128)} %bitcast.2, f32[]{:T(128)} %bitcast.1, f32[]{:T(128)} %bitcast), kind=kLoop, calls=%fused_computation.48 | loop fusion | flops 3145728 | bytes 1048608 | tf_op jit(solution)/shard_map/add | solution.py:72
  17.4 0.1 broadcast_select_fusion.1
  17.5 0.1 broadcast_select_fusion
  17.7 1.7 %collective-permute-done = f32[4,1,128,256]{3,2,1,0:T(8,128)S(1)} collective-permute-done((f32[4,1,128,256]{3,2,1,0:T(8,128)S(1)}, f32[4,1,128,256]{3,2,1,0:T(8,128)S(1)}, u32[]{:S(2)}, u32[]{:S(2)}) %collective-permute-start) | collective-permute-done | bytes 524320 | tf_op jit(solution)/shard_map/ppermute | solution.py:21
  19.4 0.9 collective-permute-done.1
  20.2 3.0 %fusion.5 = f32[4,4,128,256]{3,2,1,0:T(8,128)S(1)} fusion(f32[4,4,128,256]{3,2,1,0:T(8,128)S(1)} %copy-done.1, f32[4,1,128,256]{3,2,1,0:T(8,128)} %collective-permute-done.1, f32[4,1,128,256]{3,2,1,0:T(8,128)S(1)} %collective-permute-done, f32[2,4,128,256]{3,2,1,0:T(8,128)S(1)} %broadcast_select_fusion, f32[2,4,128,256]{3,2,1,0:T(8,128)S(1)} %broadcast_select_fusion.1, ...), kind=kLoop, calls=%fused_computation.18 | loop fusion | flops 5767168 | bytes 7864320 | tf_op jit(solution)/shard_map/sub | solution.py:82
  23.2 0.1 fusion.30
  23.4 1.3 %collective-permute-start.2 = (f32[4,1,128,256]{3,2,1,0:T(8,128)S(1)}, f32[4,1,128,256]{3,2,1,0:T(8,128)S(1)}, u32[]{:S(2)}, u32[]{:S(2)}) collective-permute-start(f32[4,1,128,256]{3,2,1,0:T(8,128)S(1)} %get-tuple-element.17), channel_id=1, source_target_pairs={{4,0},{8,4},{12,8},{5,1},{9,5},{13,9},{6,2},{10,6},{14,10},{7,3},{... | collective-permute-start | bytes 1572872 | tf_op jit(solution)/shard_map/ppermute | solution.py:21
  24.7 4.9 %collective-permute-start.3 = (f32[4,1,128,256]{3,2,1,0:T(8,128)S(1)}, f32[4,1,128,256]{3,2,1,0:T(8,128)S(1)}, u32[]{:S(2)}, u32[]{:S(2)}) collective-permute-start(f32[4,1,128,256]{3,2,1,0:T(8,128)S(1)} %get-tuple-element.18), channel_id=1, source_target_pairs={{0,4},{4,8},{8,12},{1,5},{5,9},{9,13},{2,6},{6,10},{10,14},{3,7},{... | collective-permute-start | bytes 1572872 | tf_op jit(solution)/shard_map/ppermute | solution.py:20
  29.5 8.7 %collective-permute-done.2 = f32[4,1,128,256]{3,2,1,0:T(8,128)S(1)} collective-permute-done((f32[4,1,128,256]{3,2,1,0:T(8,128)S(1)}, f32[4,1,128,256]{3,2,1,0:T(8,128)S(1)}, u32[]{:S(2)}, u32[]{:S(2)}) %collective-permute-start.2) | collective-permute-done | bytes 524320 | tf_op jit(solution)/shard_map/ppermute | solution.py:21
  38.2 0.9 collective-permute-done.3
  39.2 2.9 %multiply_reduce_fusion.1 = (f32[4]{0:T(128)S(1)}, f32[4]{0:T(128)S(1)}, f32[4,4,128,256]{3,2,1,0:T(8,128)}) fusion(f32[4,4,128,256]{3,2,1,0:T(8,128)S(1)} %fusion.5, f32[4,1,128,256]{3,2,1,0:T(8,128)S(1)} %collective-permute-done.3, f32[4,1,128,256]{3,2,1,0:T(8,128)S(1)} %collective-permute-done.2, f32[4,128,256]{2,1,0:T(8,128)S(1)} %select_add_fusion), kind=kLoop, calls=%fused_computation.43 | loop fusion | flops 6815736 | bytes 5767200 | tf_op jit(solution)/shard_map/reduce_sum | solution.py:55
  42.0 10.2 %all-reduce.3 = (f32[4]{0:T(128)S(1)}, f32[4]{0:T(128)S(1)}) all-reduce(f32[4]{0:T(128)S(1)} %get-tuple-element.7, f32[4]{0:T(128)S(1)} %get-tuple-element.6), channel_id=1, replica_groups=mesh['recon'=2,'space'=4,'grp'=4] {'space'}, use_global_device_ids=true, to_apply=%region_1.2 | all-reduce | flops 8 | bytes 64 | tf_op jit(solution)/shard_map/psum | solution.py:55
  52.3 2.1 %multiply_reduce_fusion = f32[4]{0:T(128)S(1)} fusion(f32[4,4,128,256]{3,2,1,0:T(8,128)S(1)} %fusion.5, f32[4,4,128,256]{3,2,1,0:T(8,128)} %get-tuple-element.12, f32[4]{0:T(128)S(1)} %div.36), kind=kLoop, calls=%fused_computation.41 | loop fusion | flops 2097148 | bytes 4194336 | tf_op jit(solution)/shard_map/reduce_sum | solution.py:55
  54.4 6.6 %psum.30 = f32[4]{0:T(128)S(1)} all-reduce(f32[4]{0:T(128)S(1)} %multiply_reduce_fusion), channel_id=1, replica_groups=mesh['recon'=2,'space'=4,'grp'=4] {'space'}, use_global_device_ids=true, to_apply=%region_5.6 | all-reduce | flops 4 | bytes 32 | tf_op jit(solution)/shard_map/psum | solution.py:55
  61.0 2.0 %multiply_add_fusion.1 = f32[4,4,128,256]{3,2,1,0:T(8,128)S(1)} fusion(f32[4,4,128,256]{3,2,1,0:T(8,128)S(1)} %fusion.5, f32[4,4,128,256]{3,2,1,0:T(8,128)} %get-tuple-element.12, f32[4]{0:T(128)S(1)} %div.37, f32[4]{0:T(128)S(1)} %div.36), kind=kLoop, calls=%fused_computation.40 | loop fusion | flops 2097152 | bytes 6291488 | tf_op jit(solution)/shard_map/add | solution.py:92
  62.9 0.1 fusion.29
  63.1 1.3 %collective-permute-start.4 = (f32[4,1,128,256]{3,2,1,0:T(8,128)S(1)}, f32[4,1,128,256]{3,2,1,0:T(8,128)S(1)}, u32[]{:S(2)}, u32[]{:S(2)}) collective-permute-start(f32[4,1,128,256]{3,2,1,0:T(8,128)S(1)} %get-tuple-element.15), channel_id=1, source_target_pairs={{4,0},{8,4},{12,8},{5,1},{9,5},{13,9},{6,2},{10,6},{14,10},{7,3},{... | collective-permute-start | bytes 1572872 | tf_op jit(solution)/shard_map/ppermute | solution.py:21
  64.4 4.1 %collective-permute-start.5 = (f32[4,1,128,256]{3,2,1,0:T(8,128)S(1)}, f32[4,1,128,256]{3,2,1,0:T(8,128)S(1)}, u32[]{:S(2)}, u32[]{:S(2)}) collective-permute-start(f32[4,1,128,256]{3,2,1,0:T(8,128)S(1)} %get-tuple-element.16), channel_id=1, source_target_pairs={{0,4},{4,8},{8,12},{1,5},{5,9},{9,13},{2,6},{6,10},{10,14},{3,7},{... | collective-permute-start | bytes 1572872 | tf_op jit(solution)/shard_map/ppermute | solution.py:20
  68.5 4.6 %collective-permute-done.4 = f32[4,1,128,256]{3,2,1,0:T(8,128)S(1)} collective-permute-done((f32[4,1,128,256]{3,2,1,0:T(8,128)S(1)}, f32[4,1,128,256]{3,2,1,0:T(8,128)S(1)}, u32[]{:S(2)}, u32[]{:S(2)}) %collective-permute-start.4) | collective-permute-done | bytes 524320 | tf_op jit(solution)/shard_map/ppermute | solution.py:21
  73.1 1.5 %collective-permute-done.5 = f32[4,1,128,256]{3,2,1,0:T(8,128)S(1)} collective-permute-done((f32[4,1,128,256]{3,2,1,0:T(8,128)S(1)}, f32[4,1,128,256]{3,2,1,0:T(8,128)S(1)}, u32[]{:S(2)}, u32[]{:S(2)}) %collective-permute-start.5) | collective-permute-done | bytes 524320 | tf_op jit(solution)/shard_map/ppermute | solution.py:20
  74.6 1.8 %fusion.20 = f32[4]{0:T(128)S(1)} fusion(f32[4,4,128,256]{3,2,1,0:T(8,128)S(1)} %multiply_add_fusion.1, f32[4,1,128,256]{3,2,1,0:T(8,128)S(1)} %collective-permute-done.5, f32[4,1,128,256]{3,2,1,0:T(8,128)S(1)} %collective-permute-done.4, f32[4,128,256]{2,1,0:T(8,128)S(1)} %select_add_fusion), kind=kLoop, calls=%fused_computation.45 | loop fusion | flops 5767164 | bytes 3670032 | tf_op jit(solution)/shard_map/reduce_sum | solution.py:55
  76.3 9.6 %psum.31 = f32[4]{0:T(128)S(1)} all-reduce(f32[4]{0:T(128)S(1)} %fusion.20), channel_id=1, replica_groups=mesh['recon'=2,'space'=4,'grp'=4] {'space'}, use_global_device_ids=true, to_apply=%region_7.8 | all-reduce | flops 4 | bytes 32 | tf_op jit(solution)/shard_map/psum | solution.py:55
  85.9 4.2 %fusion.26 = (bf16[4,4,128,256]{3,2,1,0:T(8,128)(2,1)S(1)}, f32[4,4,128,256]{3,2,1,0:T(8,128)}) fusion(f32[4,4,128,256]{3,2,1,0:T(8,128)S(1)} %fusion.5, f32[4]{0:T(128)S(1)} %div.37, f32[4,4,128,256]{3,2,1,0:T(8,128)} %get-tuple-element.12, f32[4]{0:T(128)S(1)} %div.38, f32[4,4,128,256]{3,2,1,0:T(8,128)} %copy-done, f32[4]{0:T(128)S(1)} %div.36), kind=kLoop, calls=%fused_computation.76 | loop fusion | flops 4718592 | bytes 9437232 | tf_op jit(solution)/shard_map/convert_element_type | solution.py:97
  90.1 1.8 %copy.17 = bf16[4,4,128,256]{3,1,0,2:T(4,128)(2,1)} copy(bf16[4,4,128,256]{3,2,1,0:T(8,128)(2,1)S(1)} %get-tuple-element.10) | data formatting | bytes 2097152 | tf_op jit(solution)/shard_map/convert_element_type | solution.py:97
  91.9 13.5 %all-to-all-start = ((bf16[4,4,128,256]{3,1,0,2:T(4,128)(2,1)}), bf16[4,4,128,256]{3,1,0,2:T(4,128)(2,1)S(1)}, u32[]{:S(2)}, u32[]{:S(2)}) async-start(bf16[4,4,128,256]{3,1,0,2:T(4,128)(2,1)} %copy.17), calls=%async_computation | async-start | bytes 2097152 | tf_op jit(solution)/shard_map/all_to_all | solution.py:98
  105.4 1.5 %fusion.28 = (f32[2,4,128,256]{3,2,1,0:T(8,128)}, f32[2,4,128,256]{3,2,1,0:T(8,128)}) fusion(f32[4,4,128,256]{3,2,1,0:T(8,128)S(1)} %copy-done.2), kind=kLoop, calls=%fused_computation.77 | loop fusion | bytes 4194304 | tf_op jit(solution)/shard_map/slice | solution.py:95
  107.0 12.1 %all-to-all-done = bf16[4,4,128,256]{3,1,0,2:T(4,128)(2,1)S(1)} async-done(((bf16[4,4,128,256]{3,1,0,2:T(4,128)(2,1)}), bf16[4,4,128,256]{3,1,0,2:T(4,128)(2,1)S(1)}, u32[]{:S(2)}, u32[]{:S(2)}) %all-to-all-start) | async-done | bytes 1048608 | tf_op jit(solution)/shard_map/all_to_all | solution.py:98
  119.0 0.4 copy.18
  119.4 0.8 reshape.129
  120.2 0.7 fusion.32
  120.9 0.2 reshape.130
  121.1 0.7 reshape.131
  121.9 0.4 fusion.21
  122.3 0.7 neg.8
  (24 shorter events, 0.2 us)
Async XLA Ops:
  0.6 1.5 %copy-start.3 = (f32[2,4,128,256]{3,2,1,0:T(8,128)S(1)}, f32[2,4,128,256]{3,2,1,0:T(8,128)}, u32[]{:S(2)}) copy-start(f32[2,4,128,256]{3,2,1,0:T(8,128)} %param.8) | copy-start | bytes 3145732
  2.2 8.3 %copy-start.7 = (s32[2]{0:T(128)S(1)}, s32[2]{0:T(128)}, u32[]{:S(2)}) copy-start(s32[2]{0:T(128)} %param.9) | copy-start | bytes 28
  2.2 8.3 %copy-start.8 = (s32[2]{0:T(128)S(1)}, s32[2]{0:T(128)}, u32[]{:S(2)}) copy-start(s32[2]{0:T(128)} %param.10) | copy-start | bytes 28
  2.2 8.6 %copy-start.5 = (f32[8]{0:T(128)S(1)}, f32[8]{0:T(128)}, u32[]{:S(2)}) copy-start(f32[8]{0:T(128)} %param.12) | copy-start | bytes 100
  2.2 9.5 %copy-start.4 = (s32[4,128,256]{2,1,0:T(8,128)S(1)}, s32[4,128,256]{2,1,0:T(8,128)}, u32[]{:S(2)}) copy-start(s32[4,128,256]{2,1,0:T(8,128)} %param.11) | copy-start | bytes 1572868
  2.3 1.3 %copy-start = (f32[4,4,128,256]{3,2,1,0:T(8,128)}, f32[4,4,128,256]{3,2,1,0:T(8,128)S(1)}, u32[]{:S(2)}) copy-start(f32[4,4,128,256]{3,2,1,0:T(8,128)S(1)} %constant_dynamic-update-slice_fusion) | copy-start | bytes 6291460
  3.7 15.7 %collective-permute-start = (f32[4,1,128,256]{3,2,1,0:T(8,128)S(1)}, f32[4,1,128,256]{3,2,1,0:T(8,128)S(1)}, u32[]{:S(2)}, u32[]{:S(2)}) collective-permute-start(f32[4,1,128,256]{3,2,1,0:T(8,128)S(1)} %get-tuple-element.19), channel_id=1, source_target_pairs={{4,0},{8,4},{12,8},{5,1},{9,5},{13,9},{6,2},{10,6},{14,10},{7,3},{... | collective-permute-start | bytes 1572872 | tf_op jit(solution)/shard_map/ppermute | solution.py:21
  5.0 15.2 %collective-permute-start.1 = (f32[4,1,128,256]{3,2,1,0:T(8,128)S(1)}, f32[4,1,128,256]{3,2,1,0:T(8,128)}, u32[]{:S(2)}, u32[]{:S(2)}) collective-permute-start(f32[4,1,128,256]{3,2,1,0:T(8,128)S(1)} %get-tuple-element.20), channel_id=1, source_target_pairs={{0,4},{4,8},{8,12},{1,5},{5,9},{9,13},{2,6},{6,10},{10,14},{3,7},{... | collective-permute-start | bytes 1572872 | tf_op jit(solution)/shard_map/ppermute | solution.py:20
  10.5 9.8 %copy-start.1 = (f32[4,4,128,256]{3,2,1,0:T(8,128)S(1)}, f32[4,4,128,256]{3,2,1,0:T(8,128)}, u32[]{:S(2)}) copy-start(f32[4,4,128,256]{3,2,1,0:T(8,128)} %copy-done) | copy-start | bytes 6291460
  23.4 14.9 %collective-permute-start.2 = (f32[4,1,128,256]{3,2,1,0:T(8,128)S(1)}, f32[4,1,128,256]{3,2,1,0:T(8,128)S(1)}, u32[]{:S(2)}, u32[]{:S(2)}) collective-permute-start(f32[4,1,128,256]{3,2,1,0:T(8,128)S(1)} %get-tuple-element.17), channel_id=1, source_target_pairs={{4,0},{8,4},{12,8},{5,1},{9,5},{13,9},{6,2},{10,6},{14,10},{7,3},{... | collective-permute-start | bytes 1572872 | tf_op jit(solution)/shard_map/ppermute | solution.py:21
  24.7 14.5 %collective-permute-start.3 = (f32[4,1,128,256]{3,2,1,0:T(8,128)S(1)}, f32[4,1,128,256]{3,2,1,0:T(8,128)S(1)}, u32[]{:S(2)}, u32[]{:S(2)}) collective-permute-start(f32[4,1,128,256]{3,2,1,0:T(8,128)S(1)} %get-tuple-element.18), channel_id=1, source_target_pairs={{0,4},{4,8},{8,12},{1,5},{5,9},{9,13},{2,6},{6,10},{10,14},{3,7},{... | collective-permute-start | bytes 1572872 | tf_op jit(solution)/shard_map/ppermute | solution.py:20
  63.1 10.0 %collective-permute-start.4 = (f32[4,1,128,256]{3,2,1,0:T(8,128)S(1)}, f32[4,1,128,256]{3,2,1,0:T(8,128)S(1)}, u32[]{:S(2)}, u32[]{:S(2)}) collective-permute-start(f32[4,1,128,256]{3,2,1,0:T(8,128)S(1)} %get-tuple-element.15), channel_id=1, source_target_pairs={{4,0},{8,4},{12,8},{5,1},{9,5},{13,9},{6,2},{10,6},{14,10},{7,3},{... | collective-permute-start | bytes 1572872 | tf_op jit(solution)/shard_map/ppermute | solution.py:21
  64.4 10.2 %collective-permute-start.5 = (f32[4,1,128,256]{3,2,1,0:T(8,128)S(1)}, f32[4,1,128,256]{3,2,1,0:T(8,128)S(1)}, u32[]{:S(2)}, u32[]{:S(2)}) collective-permute-start(f32[4,1,128,256]{3,2,1,0:T(8,128)S(1)} %get-tuple-element.16), channel_id=1, source_target_pairs={{0,4},{4,8},{8,12},{1,5},{5,9},{9,13},{2,6},{6,10},{10,14},{3,7},{... | collective-permute-start | bytes 1572872 | tf_op jit(solution)/shard_map/ppermute | solution.py:20
  90.1 15.3 %copy-start.2 = (f32[4,4,128,256]{3,2,1,0:T(8,128)S(1)}, f32[4,4,128,256]{3,2,1,0:T(8,128)}, u32[]{:S(2)}) copy-start(f32[4,4,128,256]{3,2,1,0:T(8,128)} %get-tuple-element.11) | copy-start | bytes 6291460
  91.9 27.1 %all-to-all-start = ((bf16[4,4,128,256]{3,1,0,2:T(4,128)(2,1)}), bf16[4,4,128,256]{3,1,0,2:T(4,128)(2,1)S(1)}, u32[]{:S(2)}, u32[]{:S(2)}) async-start(bf16[4,4,128,256]{3,1,0,2:T(4,128)(2,1)} %copy.17), calls=%async_computation | async-start | bytes 2097152 | tf_op jit(solution)/shard_map/all_to_all | solution.py:98
  120.9 1.0 copy-start.6
where the time goes:
time: 124 us; the launch traced here: 123 us
  starting transfers between devices  31.8 us (26%)
  waiting for transfers between devices  30.3 us (24%)
  blocking collectives  26.4 us (21%)
  other arithmetic  23.1 us (19%)
  local copies, waits for them, and re-layouts  10 us (8%)
    psum x3, blocking collectives, inner_sums(): return lax.psum(jnp.sum(first * second, axis=(1, 2, 3)), 'space')  26.4 us
    ppermute x3, waiting for transfers between devices, with_halo(): after = lax.ppermute(initial, axis, down)  15 us
    ppermute x3, starting transfers between devices, with_halo(): before = lax.ppermute(last, axis, up)  14.5 us
    all_to_all x1, starting transfers between devices, local(): lax.all_to_all(packed, 'grp', split_axis=2, concat_axis=0, tiled=True)  13.5 us
    all_to_all x1, waiting for transfers between devices, local(): lax.all_to_all(packed, 'grp', split_axis=2, concat_axis=0, tiled=True)  12.1 us
    reduce_sum x3, other arithmetic, inner_sums(): return lax.psum(jnp.sum(first * second, axis=(1, 2, 3)), 'space')  6.74 us
    add x1, other arithmetic, local(): diagonal + jnp.where(labels == region, absorption[region], jnp.float32(0.0))  5.72 us
    convert_element_type x1, other arithmetic, local(): packed = fields.astype(jnp.bfloat16)  4.23 us
  transfers between devices with their start and end apart: 7, of which 7 were waited for; matrix products, arithmetic and copies ran while one was open for 7% of the time, Pallas kernels for 0%

commit v1 on v0

v1 whole, which is shorter than its diff:
```python
import functools

import jax
import jax.numpy as jnp
from jax import lax
from jax.experimental import pallas as pl
from jax.experimental.pallas import tpu as pltpu
from jax.sharding import PartitionSpec as P

source_power = 50.0
code_scale = 1.0 / 1024.0
PAD = 8
ROWS = 32
MESH = pl.DeviceIdType.MESH


def each(count, body):
    if count <= 8:
        for i in range(count):
            body(i)
    else:
        lax.fori_loop(0, count, lambda i, c: (body(i), c)[1], 0)


def kernel(
    n_space, n_grp,
    src_pos, det_pos, absorption, codes, warm_sources, warm_detectors, labels,
    out_sources, out_detectors, out_gradient,
    x, v0, v1, diag, lab, halo_send, halo_recv, half_send, half_recv,
    parts, packed, gathered, mixed,
    load_sem, store_sem, halo_ssem, halo_rsem, part_ssem, part_rsem, a2a_ssem, a2a_rsem,
):
    f32, bf16 = jnp.float32, jnp.bfloat16
    n_src, planes, breadth, extent = warm_sources.shape
    n_det = warm_detectors.shape[0]
    n_fields = n_src + n_det
    half = breadth // 2
    owned = breadth // n_grp
    k = lax.axis_index("space")
    g = lax.axis_index("grp")
    has_down, has_up = k > 0, k < n_space - 1
    chunks = breadth // ROWS

    barrier = pltpu.get_barrier_semaphore()

    def greet_space(j):
        pl.semaphore_signal(barrier, inc=1, device_id={"space": lax.rem(k + 1 + j, n_space)}, device_id_type=MESH)

    def greet_grp(j):
        pl.semaphore_signal(barrier, inc=1, device_id={"grp": lax.rem(g + 1 + j, n_grp)}, device_id_type=MESH)

    each(n_space - 1, greet_space)
    each(n_grp - 1, greet_grp)

    def warm(f):
        return warm_detectors.at[f] if f < n_det else warm_sources.at[f - n_det]

    def out(f):
        return out_detectors.at[f] if f < n_det else out_sources.at[f - n_det]

    inner = pl.ds(PAD, breadth)
    loads = [
        pltpu.make_async_copy(warm(f), x.at[f, pl.ds(1, planes), inner], load_sem.at[f]) for f in range(n_fields)
    ]
    load_labels = pltpu.make_async_copy(labels, lab, load_sem.at[n_fields])
    loads[0].start()
    loads[1].start()
    load_labels.start()
    for f in range(2, n_fields):
        loads[f].start()

    border = jnp.zeros((PAD, extent), f32)
    for f in range(n_fields):
        for z in range(1, planes + 1):
            for buf in (x, v0, v1):
                buf[f, z, pl.ds(0, PAD)] = border
                buf[f, z, pl.ds(PAD + breadth, PAD)] = border

    def clear(side):
        halo_recv[:, :, side] = jnp.zeros((2, n_fields, breadth, extent), bf16)
        half_recv[:, side] = jnp.zeros((n_fields, half, extent), bf16)

    pl.when(jnp.logical_not(has_down))(lambda: clear(0))
    pl.when(jnp.logical_not(has_up))(lambda: clear(1))

    def halo_copy(stage, f, up):
        send, recv = (halo_send, halo_recv) if stage < 2 else (half_send, half_recv)
        at = (stage, f) if stage < 2 else (f,)
        return pltpu.make_async_remote_copy(
            src_ref=send.at[(*at, 1 if up else 0)],
            dst_ref=recv.at[(*at, 0 if up else 1)],
            send_sem=halo_ssem.at[stage, f, 1 if up else 0],
            recv_sem=halo_rsem.at[stage, f, 0 if up else 1],
            device_id={"space": k + 1 if up else k - 1},
            device_id_type=MESH,
        )

    def halo_start(stage, f):
        pl.when(has_up)(lambda: halo_copy(stage, f, True).start())
        pl.when(has_down)(lambda: halo_copy(stage, f, False).start())

    def halo_wait(stage, f):
        pl.when(has_down)(lambda: halo_copy(stage, f, True).wait_recv())
        pl.when(has_up)(lambda: halo_copy(stage, f, False).wait_recv())

    def halo_done(stage, f):
        pl.when(has_up)(lambda: halo_copy(stage, f, True).wait_send())
        pl.when(has_down)(lambda: halo_copy(stage, f, False).wait_send())

    def loop(body, carry):
        return lax.fori_loop(0, chunks, lambda i, c: body(pl.multiple_of(i * ROWS, ROWS), c), carry)

    col = lax.broadcasted_iota(jnp.int32, (ROWS, extent), 1)
    row = lax.broadcasted_iota(jnp.int32, (ROWS, extent), 0)
    first_col, last_col = col == 0, col == extent - 1

    def right(value):
        return jnp.where(first_col, 0.0, pltpu.roll(value, 1, 1))

    def left(value):
        return jnp.where(last_col, 0.0, pltpu.roll(value, extent - 1, 1))

    def window(buf, f, z, r):
        wide = buf[f, z, pl.ds(r, ROWS + 2 * PAD)]
        centre = wide[PAD:PAD + ROWS]
        after = wide[PAD + 1:PAD + ROWS + 1]
        before = wide[PAD - 1:PAD + ROWS - 1]
        return centre, before, after

    def applied(buf, f, z, r):
        centre, before, after = window(buf, f, z, r)
        beside = buf[f, z - 1, pl.ds(PAD + r, ROWS)] + buf[f, z + 1, pl.ds(PAD + r, ROWS)]
        beside = beside + before + after + right(centre) + left(centre)
        return centre, diag[z - 1, pl.ds(r, ROWS)] * centre - beside

    def fold(value):
        return jnp.sum(value.reshape(value.shape[0] // 8, 8, extent), axis=0)

    def unpack_halo(stage, buf, f):
        def body(r, c):
            buf[f, 0, pl.ds(PAD + r, ROWS)] = halo_recv[stage, f, 0, pl.ds(r, ROWS)].astype(f32)
            buf[f, planes + 1, pl.ds(PAD + r, ROWS)] = halo_recv[stage, f, 1, pl.ds(r, ROWS)].astype(f32)
            return c
        loop(body, 0)

    def make_diagonal():
        load_labels.wait()
        values = [absorption[i] for i in range(absorption.shape[0])]

        def body(r, c):
            for z in range(planes):
                label = lab[z, pl.ds(r, ROWS)]
                value = jnp.full((ROWS, extent), values[0], f32)
                for region in range(1, len(values)):
                    value = jnp.where(label == region, values[region], value)
                diag[z, pl.ds(r, ROWS)] = 6.0 + value
            return c
        loop(body, 0)

    zero = jnp.zeros((8, extent), f32)
    sums = [None] * n_fields

    def pack_start(f):
        loads[f].wait()

        def body(r, c):
            halo_send[0, f, 0, pl.ds(r, ROWS)] = x[f, 1, pl.ds(PAD + r, ROWS)].astype(bf16)
            halo_send[0, f, 1, pl.ds(r, ROWS)] = x[f, planes, pl.ds(PAD + r, ROWS)].astype(bf16)
            return c
        loop(body, 0)

    def stage0(f):
        pack_start(f)
        halo_start(0, f)

    ends, middle = (1, planes), tuple(range(2, planes))
    face = [breadth - 1] * n_det + [0] * n_src

    def residual(f, zs, send, acc):
        position = det_pos[f] if f < n_det else src_pos[f - n_det]

        def body(r, acc):
            on_face = row + r == face[f]
            for z in zs:
                code = (k * planes + (z - 1)) * extent + col
                drive = jnp.where(on_face & (code == position), source_power, 0.0)
                value = drive - applied(x, f, z, r)[1]
                v0[f, z, pl.ds(PAD + r, ROWS)] = value
                if send and z == 1:
                    halo_send[1, f, 0, pl.ds(r, ROWS)] = value.astype(bf16)
                if send and z == planes:
                    halo_send[1, f, 1, pl.ds(r, ROWS)] = value.astype(bf16)
                acc = acc + fold(value * value)
            return acc
        return loop(body, acc)

    def stage1(f):
        acc = residual(f, middle, False, zero)
        halo_wait(0, f)
        unpack_halo(0, x, f)
        acc = residual(f, ends, True, acc)
        halo_start(1, f)
        sums[f] = (acc,)

    def second(f, zs, acc):
        def body(r, acc):
            m01, m11 = acc
            for z in zs:
                centre, value = applied(v0, f, z, r)
                v1[f, z, pl.ds(PAD + r, ROWS)] = value
                m01 = m01 + fold(centre * value)
                m11 = m11 + fold(value * value)
            return m01, m11
        return loop(body, acc)

    def stage2(f):
        acc = second(f, middle, (zero, zero))
        halo_wait(1, f)
        unpack_halo(1, v0, f)
        acc = second(f, ends, acc)
        half_send[f, 0] = v1[f, 1, pl.ds(PAD + half, half)].astype(bf16)
        half_send[f, 1] = v1[f, planes, pl.ds(PAD, half)].astype(bf16)
        halo_start(2, f)

        def body(r, m12):
            for z in range(1, planes + 1):
                centre, _, after = window(v1, f, z, r)
                beside = after + right(centre)
                if z < planes:
                    beside = beside + v1[f, z + 1, pl.ds(PAD + r, ROWS)]
                m12 = m12 + fold(centre * (diag[z - 1, pl.ds(r, ROWS)] * centre - 2.0 * beside))
            return m12
        sums[f] = (*sums[f], *acc, loop(body, zero))

    def part_copy(f, mine, peer):
        return pltpu.make_async_remote_copy(
            src_ref=parts.at[f, mine],
            dst_ref=parts.at[f, mine],
            send_sem=part_ssem.at[f, peer],
            recv_sem=part_rsem.at[f, mine],
            device_id={"space": peer},
            device_id_type=MESH,
        )

    def stage3(f):
        halo_wait(2, f)
        m00, m01, m11, m12 = sums[f]
        below = half_recv[f, 0].astype(f32) * v1[f, 1, pl.ds(PAD, half)]
        above = half_recv[f, 1].astype(f32) * v1[f, planes, pl.ds(PAD + half, half)]
        m12 = m12 - 2.0 * fold(below + above)
        which = lax.broadcasted_iota(jnp.int32, (8, 128), 0)
        tile = jnp.zeros((8, 128), f32)
        for j, m in enumerate((m00, m01, m11, m12)):
            m = jnp.sum(m, axis=0, keepdims=True)
            total = m[:, :128]
            for lane in range(128, extent, 128):
                total = total + m[:, lane:lane + 128]
            tile = jnp.where(which == j, total, tile)
        parts[f, k] = tile
        each(n_space - 1, lambda j: part_copy(f, k, lax.rem(k + 1 + j, n_space)).start())

    def a2a_copy(f, owner, peer):
        return pltpu.make_async_remote_copy(
            src_ref=packed.at[f, :, pl.ds(pl.multiple_of(peer * owned, owned), owned)],
            dst_ref=gathered.at[f, owner],
            send_sem=a2a_ssem.at[f, peer],
            recv_sem=a2a_rsem.at[f, owner],
            device_id={"grp": peer},
            device_id_type=MESH,
        )

    def stage4(f):
        each(n_space - 1, lambda j: part_copy(f, lax.rem(k + 1 + j, n_space), k).wait_recv())
        if n_space <= 8:
            total = parts[f, 0]
            for j in range(1, n_space):
                total = total + parts[f, j]
        else:
            total = lax.fori_loop(0, n_space, lambda j, t: t + parts[f, j], jnp.zeros((8, 128), f32))
        total = jnp.sum(total, axis=1, keepdims=True)
        m00, m01, m11, m12 = (total[j:j + 1] for j in range(4))
        alpha0 = m00 / m01
        norm1 = jnp.maximum(alpha0 * alpha0 * m11 - m00, 0.0)
        more = 1.0 + norm1 / m00
        curve = more * more * m01 - 2.0 * more * alpha0 * m11 + alpha0 * alpha0 * m12
        alpha1 = jnp.minimum(jnp.maximum(norm1 / curve, 1.0 / 12.7), 1.0 / 0.0199)
        c0 = alpha0 + alpha1 * more
        c1 = -alpha1 * alpha0

        def body(r, c):
            for z in range(1, planes + 1):
                rows = pl.ds(PAD + r, ROWS)
                value = x[f, z, rows] + c0 * v0[f, z, rows] + c1 * v1[f, z, rows]
                x[f, z, rows] = value
                packed[f, z - 1, pl.ds(r, ROWS)] = value.astype(bf16)
            return c
        loop(body, 0)
        each(n_grp - 1, lambda j: a2a_copy(f, g, lax.rem(g + 1 + j, n_grp)).start())
        pltpu.make_async_copy(x.at[f, pl.ds(1, planes), inner], out(f), store_sem.at[f]).start()
        gathered[f, g] = packed[f, :, pl.ds(pl.multiple_of(g * owned, owned), owned)]

    def stage5(f):
        each(n_grp - 1, lambda j: a2a_copy(f, lax.rem(g + 1 + j, n_grp), g).wait_recv())
        if f < n_det - 1:
            return
        step = 16
        if f == n_det - 1:
            def body(i, c):
                r = pl.multiple_of(i * step, step)
                for z in range(planes):
                    held = [
                        gathered[d % n_det, d // n_det, z, pl.ds(r, step)].astype(f32) for d in range(n_grp * n_det)
                    ]
                    for s in range(n_grp * n_src):
                        total = held[0] * (codes[s, 0].astype(f32) * code_scale)
                        for d in range(1, n_grp * n_det):
                            total = total + held[d] * (codes[s, d].astype(f32) * code_scale)
                        mixed[s, z, pl.ds(r, step)] = total
                return c
            lax.fori_loop(0, owned // step, body, 0)
            return

        def body(i, c):
            r = pl.multiple_of(i * step, step)
            for z in range(planes):
                total = jnp.zeros((step, extent), f32)
                for q in range(n_grp):
                    total = total - gathered[f, q, z, pl.ds(r, step)].astype(f32) * mixed[
                        q * n_src + f - n_det, z, pl.ds(r, step)
                    ]
                if f > n_det:
                    total = total + out_gradient[z, pl.ds(r, step)]
                out_gradient[z, pl.ds(r, step)] = total
            return c
        lax.fori_loop(0, owned // step, body, 0)

    pack_start(0)
    pack_start(1)
    pl.semaphore_wait(barrier, n_space - 1 + n_grp - 1)
    halo_start(0, 0)
    halo_start(0, 1)
    make_diagonal()

    stages = (stage0, stage1, stage2, stage3, stage4, stage5)
    for t in range(1, n_fields + 6):
        if 1 < t < n_fields:
            stage0(t)
        for s in range(5, 0, -1):
            if 0 <= t - s < n_fields:
                stages[s](t - s)

    for f in range(n_fields):
        for stage in range(3):
            halo_done(stage, f)
        each(n_space - 1, lambda j: part_copy(f, k, lax.rem(k + 1 + j, n_space)).wait_send())
        each(n_grp - 1, lambda j: a2a_copy(f, g, lax.rem(g + 1 + j, n_grp)).wait_send())
        pltpu.make_async_copy(x.at[f, pl.ds(1, planes), inner], out(f), store_sem.at[f]).wait()


def solution(mesh):
    n_space, n_grp = mesh.shape["space"], mesh.shape["grp"]

    def local(warm_sources, warm_detectors, source_positions, detector_positions, labels, absorption, residual_codes):
        n_src, planes, breadth, extent = warm_sources.shape
        n_det = warm_detectors.shape[0]
        n = n_src + n_det
        owned = breadth // n_grp
        f32, bf16 = jnp.float32, jnp.bfloat16
        smem = pl.BlockSpec(memory_space=pltpu.SMEM)
        hbm = pl.BlockSpec(memory_space=pl.ANY)
        vmem = pl.BlockSpec(memory_space=pltpu.VMEM)
        sem = pltpu.SemaphoreType.DMA
        tall = (n, planes + 2, breadth + 2 * PAD, extent)
        return pl.pallas_call(
            functools.partial(kernel, n_space, n_grp),
            out_shape=(
                jax.ShapeDtypeStruct(warm_sources.shape, f32),
                jax.ShapeDtypeStruct(warm_detectors.shape, f32),
                jax.ShapeDtypeStruct((planes, owned, extent), f32),
            ),
            in_specs=[smem] * 4 + [hbm] * 3,
            out_specs=(hbm, hbm, vmem),
            scratch_shapes=[
                pltpu.VMEM(tall, f32),
                pltpu.VMEM(tall, f32),
                pltpu.VMEM(tall, f32),
                pltpu.VMEM((planes, breadth, extent), f32),
                pltpu.VMEM((planes, breadth, extent), jnp.int32),
                pltpu.VMEM((2, n, 2, breadth, extent), bf16),
                pltpu.VMEM((2, n, 2, breadth, extent), bf16),
                pltpu.VMEM((n, 2, breadth // 2, extent), bf16),
                pltpu.VMEM((n, 2, breadth // 2, extent), bf16),
                pltpu.VMEM((n, n_space, 8, 128), f32),
                pltpu.VMEM((n, planes, breadth, extent), bf16),
                pltpu.VMEM((n, n_grp, planes, owned, extent), bf16),
                pltpu.VMEM((n_grp * n_src, planes, owned, extent), f32),
                sem((n + 1,)),
                sem((n,)),
                sem((3, n, 2)),
                sem((3, n, 2)),
                sem((n, n_space)),
                sem((n, n_space)),
                sem((n, n_grp)),
                sem((n, n_grp)),
            ],
            compiler_params=pltpu.CompilerParams(
                collective_id=0, has_side_effects=True, vmem_limit_bytes=40 * 1024 * 1024
            ),
        )(source_positions, detector_positions, absorption, residual_codes, warm_sources, warm_detectors, labels)

    fields = P(("recon", "grp"), "space", None, None)
    return jax.shard_map(
        local,
        mesh=mesh,
        in_specs=(
            fields,
            fields,
            P(("recon", "grp")),
            P(("recon", "grp")),
            P(("recon", "space"), None, None),
            P(),
            P("recon", None),
        ),
        out_specs=(fields, fields, P(("recon", "space"), "grp", None)),
        check_vma=False,
    )
```

time: 124 us -> 51.5 us (0.42)
  Pallas kernels: 0 us -> 41.8 us
  starting transfers between devices: 31.8 us -> 0 us
  waiting for transfers between devices: 30.3 us -> 0 us
  blocking collectives: 26.4 us -> 0 us
  other arithmetic: 23.1 us -> 0 us
  local copies, waits for them, and re-layouts: 10 us -> 8.73 us
    pallas_call x0 -> x1, Pallas kernels: none -> 41.8 us  [local(): pl.pallas_call(functools.partial(kernel, n_space, n_grp), out_shape=(jax....]
    psum x3 -> x0, blocking collectives: 26.4 us -> none  [inner_sums(): return lax.psum(jnp.sum(first * second, axis=(1, 2, 3)), 'space')]
    ppermute x6 -> x0, starting transfers between devices: 18.3 us -> none  [the longest x3 14.5 us: with_halo(): before = lax.ppermute(last, axis, up)]
    ppermute x6 -> x0, waiting for transfers between devices: 18.3 us -> none  [the longest x3 15 us: with_halo(): after = lax.ppermute(initial, axis, down)]
    all_to_all x1 -> x0, starting transfers between devices: 13.5 us -> none  [local(): lax.all_to_all(packed, 'grp', split_axis=2, concat_axis=0, tiled=True)]
    all_to_all x1 -> x0, waiting for transfers between devices: 12.1 us -> none  [local(): lax.all_to_all(packed, 'grp', split_axis=2, concat_axis=0, tiled=True)]
    add x2 -> x0, other arithmetic: 7.68 us -> none  [the longest x1 5.72 us: local(): diagonal + jnp.where(labels == region, absorption[region], jnp.float32(0.0))]
    reduce_sum x3 -> x0, other arithmetic: 6.74 us -> none  [inner_sums(): return lax.psum(jnp.sum(first * second, axis=(1, 2, 3)), 'space')]
  transfers between devices with their start and end apart: 7 -> 0, of which waited for: 7 -> 0; matrix products, arithmetic and copies ran while one was open for 7% -> 0% of each run, Pallas kernels for 0% -> 0%
where the time goes in v1:
time: 51.5 us; the launch traced here: 51.2 us
  Pallas kernels  41.8 us (81%)
  local copies, waits for them, and re-layouts  8.73 us (17%)
  between operations  0.66 us (1%)
    pallas_call x1, Pallas kernels, local(): pl.pallas_call(functools.partial(kernel, n_space, n_grp), out_shape=(jax....  41.8 us
    unnamed x17, local copies, waits for them, and re-layouts  8.73 us

profile of v1, /device:TPU:1, one launch (start us, length us, event | category | flops | bytes accessed | tf_op | source)
XLA Modules:
  0.0 51.2 jit_solution(5988503625599958700)
XLA Ops:
  0.6 0.0 copy-start
  0.6 1.2 %copy-done = f32[2,4,128,256]{3,2,1,0:T(8,128)S(1)} copy-done((f32[2,4,128,256]{3,2,1,0:T(8,128)S(1)}, f32[2,4,128,256]{3,2,1,0:T(8,128)}, u32[]{:S(2)}) %copy-start) | copy-done | bytes 1048600
  1.9 0.0 copy-start.1
  1.9 1.2 %copy-done.1 = f32[2,4,128,256]{3,2,1,0:T(8,128)S(1)} copy-done((f32[2,4,128,256]{3,2,1,0:T(8,128)S(1)}, f32[2,4,128,256]{3,2,1,0:T(8,128)}, u32[]{:S(2)}) %copy-start.1) | copy-done | bytes 1048600
  3.1 0.0 copy-start.2
  3.1 1.0 %copy-done.2 = s32[4,128,256]{2,1,0:T(8,128)S(1)} copy-done((s32[4,128,256]{2,1,0:T(8,128)S(1)}, s32[4,128,256]{2,1,0:T(8,128)}, u32[]{:S(2)}) %copy-start.2) | copy-done | bytes 524312
  4.1 0.0 copy-start.3
  4.1 0.7 %copy-done.3 = s32[8,8]{1,0:T(8,128)S(1)} copy-done((s32[8,8]{1,0:T(8,128)S(1)}, s32[8,8]{1,0:T(8,128)}, u32[]{:S(2)}) %copy-start.3) | copy-done | bytes 280
  4.8 0.0 copy-start.4
  4.8 0.7 %copy-done.4 = s32[2]{0:T(128)S(1)} copy-done((s32[2]{0:T(128)S(1)}, s32[2]{0:T(128)}, u32[]{:S(2)}) %copy-start.4) | copy-done | bytes 32
  5.5 0.0 copy-start.5
  5.5 0.7 %copy-done.5 = s32[2]{0:T(128)S(1)} copy-done((s32[2]{0:T(128)S(1)}, s32[2]{0:T(128)}, u32[]{:S(2)}) %copy-start.5) | copy-done | bytes 32
  6.1 0.0 copy-start.6
  6.1 0.7 %copy-done.6 = f32[8]{0:T(128)S(1)} copy-done((f32[8]{0:T(128)S(1)}, f32[8]{0:T(128)}, u32[]{:S(2)}) %copy-start.6) | copy-done | bytes 56
  6.8 41.8 %shard_map.94 = (f32[2,4,128,256]{3,2,1,0:T(8,128)S(1)}, f32[2,4,128,256]{3,2,1,0:T(8,128)S(1)}, f32[4,32,256]{2,1,0:T(8,128)S(1)}) custom-call(s32[2]{0:T(128)S(1)} %copy-done.4, s32[2]{0:T(128)S(1)} %copy-done.5, f32[8]{0:T(128)S(1)} %copy-done.6, s32[8,8]{1,0:T(8,128)S(1)} %copy-done.3, f32[2,4,128,256]{3,2,1,0:T(8,128)S(1)} %copy-done, ...), custom_call_target="tpu_custom_call" | custom-call | tf_op jit(solution)/shard_map/pallas_call | solution.py:374
  48.6 1.0 %copy.13 = f32[2,4,128,256]{3,2,1,0:T(8,128)} copy(f32[2,4,128,256]{3,2,1,0:T(8,128)S(1)} %get-tuple-element.6) | data formatting | bytes 2097152
  49.5 1.0 %copy.14 = f32[2,4,128,256]{3,2,1,0:T(8,128)} copy(f32[2,4,128,256]{3,2,1,0:T(8,128)S(1)} %get-tuple-element.7) | data formatting | bytes 2097152
  50.5 0.7 %copy.15 = f32[4,32,256]{2,1,0:T(8,128)} copy(f32[4,32,256]{2,1,0:T(8,128)S(1)} %get-tuple-element.8) | data formatting | bytes 262144
Async XLA Ops:
  0.6 1.2 %copy-start = (f32[2,4,128,256]{3,2,1,0:T(8,128)S(1)}, f32[2,4,128,256]{3,2,1,0:T(8,128)}, u32[]{:S(2)}) copy-start(f32[2,4,128,256]{3,2,1,0:T(8,128)} %warm_sources.1) | copy-start | bytes 3145732
  1.9 1.2 %copy-start.1 = (f32[2,4,128,256]{3,2,1,0:T(8,128)S(1)}, f32[2,4,128,256]{3,2,1,0:T(8,128)}, u32[]{:S(2)}) copy-start(f32[2,4,128,256]{3,2,1,0:T(8,128)} %warm_detectors.1) | copy-start | bytes 3145732
  3.1 1.0 %copy-start.2 = (s32[4,128,256]{2,1,0:T(8,128)S(1)}, s32[4,128,256]{2,1,0:T(8,128)}, u32[]{:S(2)}) copy-start(s32[4,128,256]{2,1,0:T(8,128)} %labels.1) | copy-start | bytes 1572868
  4.1 0.7 %copy-start.3 = (s32[8,8]{1,0:T(8,128)S(1)}, s32[8,8]{1,0:T(8,128)}, u32[]{:S(2)}) copy-start(s32[8,8]{1,0:T(8,128)} %codes.1) | copy-start | bytes 772
  4.8 0.7 %copy-start.4 = (s32[2]{0:T(128)S(1)}, s32[2]{0:T(128)}, u32[]{:S(2)}) copy-start(s32[2]{0:T(128)} %src_pos.1) | copy-start | bytes 28
  5.5 0.7 %copy-start.5 = (s32[2]{0:T(128)S(1)}, s32[2]{0:T(128)}, u32[]{:S(2)}) copy-start(s32[2]{0:T(128)} %det_pos.1) | copy-start | bytes 28
  6.1 0.7 %copy-start.6 = (f32[8]{0:T(128)S(1)}, f32[8]{0:T(128)}, u32[]{:S(2)}) copy-start(f32[8]{0:T(128)} %absorption.1) | copy-start | bytes 100

commit v2 on v1

v2 whole, which is shorter than its diff:
```python
import functools

import jax
import jax.numpy as jnp
from jax import lax
from jax.experimental import pallas as pl
from jax.experimental.pallas import tpu as pltpu
from jax.sharding import PartitionSpec as P

source_power = 50.0
code_scale = 1.0 / 1024.0
PAD = 8
ROWS = 32
HALO = 3
MESH = pl.DeviceIdType.MESH


def each(count, body):
    if count <= 8:
        for i in range(count):
            body(i)
    else:
        lax.fori_loop(0, count, lambda i, c: (body(i), c)[1], 0)


def kernel(
    n_space, n_grp,
    src_pos_hbm, det_pos_hbm, absorption_hbm, codes_hbm, warm_sources, warm_detectors, labels,
    out_sources, out_detectors, out_gradient,
    x, v0, v1, diag, lab, halo_send, halo_recv, lab_send, lab_recv,
    parts, packed, gathered, mixed,
    src_pos, det_pos, absorption, codes, scalar_sem,
    load_sem, store_sem, halo_ssem, halo_rsem, part_ssem, part_rsem, a2a_ssem, a2a_rsem,
):
    f32, bf16 = jnp.float32, jnp.bfloat16
    n_src, planes, breadth, extent = warm_sources.shape
    n_det = warm_detectors.shape[0]
    n_fields = n_src + n_det
    half = breadth // 2
    owned = breadth // n_grp
    k = lax.axis_index("space")
    g = lax.axis_index("grp")
    has_down, has_up = k > 0, k < n_space - 1
    chunks = breadth // ROWS

    barrier = pltpu.get_barrier_semaphore()

    def greet_space(j):
        pl.semaphore_signal(barrier, inc=1, device_id={"space": lax.rem(k + 1 + j, n_space)}, device_id_type=MESH)

    def greet_grp(j):
        pl.semaphore_signal(barrier, inc=1, device_id={"grp": lax.rem(g + 1 + j, n_grp)}, device_id_type=MESH)

    each(n_space - 1, greet_space)
    each(n_grp - 1, greet_grp)

    def warm(f):
        return warm_detectors.at[f] if f < n_det else warm_sources.at[f - n_det]

    def out(f):
        return out_detectors.at[f] if f < n_det else out_sources.at[f - n_det]

    inner = pl.ds(PAD, breadth)
    loads = [
        pltpu.make_async_copy(warm(f), x.at[f, pl.ds(HALO, planes), inner], load_sem.at[f]) for f in range(n_fields)
    ]
    load_labels = pltpu.make_async_copy(labels, lab, load_sem.at[n_fields])
    scalars = [
        pltpu.make_async_copy(a, b, scalar_sem.at[i])
        for i, (a, b) in enumerate(
            ((absorption_hbm, absorption), (src_pos_hbm, src_pos), (det_pos_hbm, det_pos), (codes_hbm, codes))
        )
    ]
    loads[0].start()
    loads[1].start()
    load_labels.start()
    for copy in scalars:
        copy.start()
    for f in range(2, n_fields):
        loads[f].start()

    border = jnp.zeros((PAD, extent), f32)
    for f in range(n_fields):
        for z in range(HALO - 2, HALO + planes + 2):
            for buf in (x, v0, v1):
                buf[f, z, pl.ds(0, PAD)] = border
                buf[f, z, pl.ds(PAD + breadth, PAD)] = border

    def clear(side):
        halo_recv[:, side] = jnp.zeros(halo_recv.shape[:1] + halo_recv.shape[2:], bf16)
        lab_recv[side] = jnp.zeros(lab_recv.shape[1:], bf16)

    pl.when(jnp.logical_not(has_down))(lambda: clear(0))
    pl.when(jnp.logical_not(has_up))(lambda: clear(1))
    inside = (jnp.where(has_down, 1.0, 0.0), jnp.where(has_up, 1.0, 0.0))

    def halo_copy(f, up):
        send, recv = (halo_send.at[f], halo_recv.at[f]) if f < n_fields else (lab_send, lab_recv)
        return pltpu.make_async_remote_copy(
            src_ref=send.at[1 if up else 0],
            dst_ref=recv.at[0 if up else 1],
            send_sem=halo_ssem.at[f, 1 if up else 0],
            recv_sem=halo_rsem.at[f, 0 if up else 1],
            device_id={"space": k + 1 if up else k - 1},
            device_id_type=MESH,
        )

    def halo_start(f):
        pl.when(has_up)(lambda: halo_copy(f, True).start())
        pl.when(has_down)(lambda: halo_copy(f, False).start())

    def halo_wait(f):
        pl.when(has_down)(lambda: halo_copy(f, True).wait_recv())
        pl.when(has_up)(lambda: halo_copy(f, False).wait_recv())

    def halo_done(f):
        pl.when(has_up)(lambda: halo_copy(f, True).wait_send())
        pl.when(has_down)(lambda: halo_copy(f, False).wait_send())

    def loop(body, carry):
        return lax.fori_loop(0, chunks, lambda i, c: body(pl.multiple_of(i * ROWS, ROWS), c), carry)

    def half_loop(body, carry):
        return lax.fori_loop(0, chunks // 2, lambda i, c: body(pl.multiple_of(i * ROWS, ROWS), c), carry)

    col = lax.broadcasted_iota(jnp.int32, (ROWS, extent), 1)
    row = lax.broadcasted_iota(jnp.int32, (ROWS, extent), 0)
    first_col, last_col = col == 0, col == extent - 1

    def right(value):
        return jnp.where(first_col, 0.0, pltpu.roll(value, 1, 1))

    def left(value):
        return jnp.where(last_col, 0.0, pltpu.roll(value, extent - 1, 1))

    def window(buf, f, z, r):
        wide = buf[f, z + HALO, pl.ds(r, ROWS + 2 * PAD)]
        centre = wide[PAD:PAD + ROWS]
        after = wide[PAD + 1:PAD + ROWS + 1]
        before = wide[PAD - 1:PAD + ROWS - 1]
        return centre, before, after

    def applied(buf, f, z, r):
        centre, before, after = window(buf, f, z, r)
        rows = pl.ds(PAD + r, ROWS)
        beside = buf[f, z + HALO - 1, rows] + buf[f, z + HALO + 1, rows]
        beside = beside + before + after + right(centre) + left(centre)
        return centre, diag[z + 2, pl.ds(r, ROWS)] * centre - beside

    def fold(value):
        return jnp.sum(value.reshape(value.shape[0] // 8, 8, extent), axis=0)

    def make_diagonal():
        for copy in scalars:
            copy.wait()
        values = [absorption[i] for i in range(absorption.shape[0])]

        def body(r, c):
            for z in range(planes):
                diag[z + 2, pl.ds(r, ROWS)] = 6.0 + looked_up(lab[z, pl.ds(r, ROWS)], values)
            return c
        loop(body, 0)
        return values

    def looked_up(label, values):
        value = jnp.full((ROWS, extent), values[0], f32)
        for region in range(1, len(values)):
            value = jnp.where(label == region, values[region], value)
        return value

    def outer_diagonal(values):
        halo_wait(n_fields)

        def body(r, c):
            for side, z in ((0, -1), (1, planes)):
                label = lab_recv[side, pl.ds(r, ROWS)].astype(f32)
                diag[z + 2, pl.ds(r, ROWS)] = 6.0 + looked_up(label, values)
            return c
        loop(body, 0)

        def half_body(r, c):
            for side, z in ((0, -2), (1, planes + 1)):
                label = lab_recv[side, pl.ds(breadth + r, ROWS)].astype(f32)
                diag[z + 2, pl.ds(side * half + r, ROWS)] = 6.0 + looked_up(label, values)
            return c
        half_loop(half_body, 0)

    def labels_start():
        load_labels.wait()

        def body(r, c):
            rows = pl.ds(r, ROWS)
            lab_send[0, rows] = lab[0, rows].astype(f32).astype(bf16)
            lab_send[1, rows] = lab[planes - 1, rows].astype(f32).astype(bf16)
            return c
        loop(body, 0)

        def half_body(r, c):
            to = pl.ds(breadth + r, ROWS)
            lab_send[0, to] = lab[1, pl.ds(half + r, ROWS)].astype(f32).astype(bf16)
            lab_send[1, to] = lab[planes - 2, pl.ds(r, ROWS)].astype(f32).astype(bf16)
            return c
        half_loop(half_body, 0)
        halo_start(n_fields)

    zero = jnp.zeros((8, extent), f32)
    sums = [None] * n_fields

    def pack(f):
        loads[f].wait()

        def body(r, c):
            rows = pl.ds(PAD + r, ROWS)
            for depth in range(2):
                to = pl.ds(depth * breadth + r, ROWS)
                halo_send[f, 0, to] = x[f, HALO + depth, rows].astype(bf16)
                halo_send[f, 1, to] = x[f, HALO + planes - 1 - depth, rows].astype(bf16)
            return c
        loop(body, 0)

        def half_body(r, c):
            to = pl.ds(2 * breadth + r, ROWS)
            halo_send[f, 0, to] = x[f, HALO + 2, pl.ds(PAD + half + r, ROWS)].astype(bf16)
            halo_send[f, 1, to] = x[f, HALO + planes - 3, pl.ds(PAD + r, ROWS)].astype(bf16)
            return c
        half_loop(half_body, 0)

    def unpack(f):
        def body(r, c):
            rows = pl.ds(PAD + r, ROWS)
            for depth in range(2):
                at = pl.ds(depth * breadth + r, ROWS)
                x[f, HALO - 1 - depth, rows] = halo_recv[f, 0, at].astype(f32)
                x[f, HALO + planes + depth, rows] = halo_recv[f, 1, at].astype(f32)
            return c
        loop(body, 0)

        def half_body(r, c):
            at = pl.ds(2 * breadth + r, ROWS)
            x[f, HALO - 3, pl.ds(PAD + r, ROWS)] = halo_recv[f, 0, at].astype(f32)
            x[f, HALO + planes + 2, pl.ds(PAD + half + r, ROWS)] = halo_recv[f, 1, at].astype(f32)
            return c
        half_loop(half_body, 0)

    face = [breadth - 1] * n_det + [0] * n_src

    def residual(f, z, r):
        position = det_pos[f] if f < n_det else src_pos[f - n_det]
        code = (k * planes + z) * extent + col
        drive = jnp.where((row + r == face[f]) & (code == position), source_power, 0.0)
        value = drive - applied(x, f, z, r)[1]
        if z < 0:
            value = value * inside[0]
        elif z >= planes:
            value = value * inside[1]
        v0[f, z + HALO, pl.ds(PAD + r, ROWS)] = value
        return value

    def stage1(f):
        def body(r, acc):
            for z in range(1, planes - 1):
                value = residual(f, z, r)
                acc = acc + fold(value * value)
            return acc
        sums[f] = loop(body, zero)

    def stage2(f):
        halo_wait(f)
        unpack(f)

        def outer(r, acc):
            for z in (0, planes - 1):
                value = residual(f, z, r)
                acc = acc + fold(value * value)
            for z in (-1, planes):
                residual(f, z, r)
            return acc
        m00 = loop(outer, sums[f])

        def outer_half(r, c):
            residual(f, -2, r)
            residual(f, planes + 1, half + r)
            return c
        half_loop(outer_half, 0)

        def image(r, acc):
            m01, m11 = acc
            for z in range(planes):
                centre, value = applied(v0, f, z, r)
                v1[f, z + HALO, pl.ds(PAD + r, ROWS)] = value
                m01 = m01 + fold(centre * value)
                m11 = m11 + fold(value * value)
            return m01, m11
        m01, m11 = loop(image, (zero, zero))

        def curvature(r, m12):
            for z in range(planes):
                centre, _, after = window(v1, f, z, r)
                beside = after + right(centre)
                if z < planes - 1:
                    beside = beside + v1[f, z + HALO + 1, pl.ds(PAD + r, ROWS)]
                m12 = m12 + fold(centre * (diag[z + 2, pl.ds(r, ROWS)] * centre - 2.0 * beside))
            return m12
        m12 = loop(curvature, zero)

        def across(r, m12):
            below = applied(v0, f, -1, r)[1] * v1[f, HALO, pl.ds(PAD + r, ROWS)]
            above = applied(v0, f, planes, half + r)[1] * v1[f, HALO + planes - 1, pl.ds(PAD + half + r, ROWS)]
            return m12 - 2.0 * fold(inside[0] * below + inside[1] * above)
        m12 = half_loop(across, m12)
        send_sums(f, m00, m01, m11, m12)

    def part_copy(f, mine, peer):
        return pltpu.make_async_remote_copy(
            src_ref=parts.at[f, mine],
            dst_ref=parts.at[f, mine],
            send_sem=part_ssem.at[f, peer],
            recv_sem=part_rsem.at[f, mine],
            device_id={"space": peer},
            device_id_type=MESH,
        )

    def send_sums(f, m00, m01, m11, m12):
        which = lax.broadcasted_iota(jnp.int32, (8, 128), 0)
        tile = jnp.zeros((8, 128), f32)
        for j, m in enumerate((m00, m01, m11, m12)):
            m = jnp.sum(m, axis=0, keepdims=True)
            total = m[:, :128]
            for lane in range(128, extent, 128):
                total = total + m[:, lane:lane + 128]
            tile = jnp.where(which == j, total, tile)
        parts[f, k] = tile
        each(n_space - 1, lambda j: part_copy(f, k, lax.rem(k + 1 + j, n_space)).start())

    def a2a_copy(f, owner, peer):
        return pltpu.make_async_remote_copy(
            src_ref=packed.at[f, :, pl.ds(pl.multiple_of(peer * owned, owned), owned)],
            dst_ref=gathered.at[f, owner],
            send_sem=a2a_ssem.at[f, peer],
            recv_sem=a2a_rsem.at[f, owner],
            device_id={"grp": peer},
            device_id_type=MESH,
        )

    def stage4(f):
        each(n_space - 1, lambda j: part_copy(f, lax.rem(k + 1 + j, n_space), k).wait_recv())
        if n_space <= 8:
            total = parts[f, 0]
            for j in range(1, n_space):
                total = total + parts[f, j]
        else:
            total = lax.fori_loop(0, n_space, lambda j, t: t + parts[f, j], jnp.zeros((8, 128), f32))
        total = jnp.sum(total, axis=1, keepdims=True)
        m00, m01, m11, m12 = (total[j:j + 1] for j in range(4))
        alpha0 = m00 / m01
        norm1 = jnp.maximum(alpha0 * alpha0 * m11 - m00, 0.0)
        more = 1.0 + norm1 / m00
        curve = more * more * m01 - 2.0 * more * alpha0 * m11 + alpha0 * alpha0 * m12
        alpha1 = jnp.minimum(jnp.maximum(norm1 / curve, 1.0 / 12.7), 1.0 / 0.0199)
        c0 = alpha0 + alpha1 * more
        c1 = -alpha1 * alpha0

        def body(r, c):
            rows = pl.ds(PAD + r, ROWS)
            for z in range(planes):
                at = (f, z + HALO, rows)
                value = x[at] + c0 * v0[at] + c1 * v1[at]
                x[at] = value
                packed[f, z, pl.ds(r, ROWS)] = value.astype(bf16)
            return c
        loop(body, 0)
        each(n_grp - 1, lambda j: a2a_copy(f, g, lax.rem(g + 1 + j, n_grp)).start())
        pltpu.make_async_copy(x.at[f, pl.ds(HALO, planes), inner], out(f), store_sem.at[f]).start()
        gathered[f, g] = packed[f, :, pl.ds(pl.multiple_of(g * owned, owned), owned)]

    def stage5(f):
        each(n_grp - 1, lambda j: a2a_copy(f, lax.rem(g + 1 + j, n_grp), g).wait_recv())
        if f < n_det - 1:
            return
        step = 16
        if f == n_det - 1:
            def body(i, c):
                r = pl.multiple_of(i * step, step)
                for z in range(planes):
                    held = [
                        gathered[d % n_det, d // n_det, z, pl.ds(r, step)].astype(f32) for d in range(n_grp * n_det)
                    ]
                    for s in range(n_grp * n_src):
                        total = held[0] * (codes[s, 0].astype(f32) * code_scale)
                        for d in range(1, n_grp * n_det):
                            total = total + held[d] * (codes[s, d].astype(f32) * code_scale)
                        mixed[s, z, pl.ds(r, step)] = total
                return c
            lax.fori_loop(0, owned // step, body, 0)
            return

        def body(i, c):
            r = pl.multiple_of(i * step, step)
            for z in range(planes):
                total = jnp.zeros((step, extent), f32)
                for q in range(n_grp):
                    total = total - gathered[f, q, z, pl.ds(r, step)].astype(f32) * mixed[
                        q * n_src + f - n_det, z, pl.ds(r, step)
                    ]
                if f > n_det:
                    total = total + out_gradient[z, pl.ds(r, step)]
                out_gradient[z, pl.ds(r, step)] = total
            return c
        lax.fori_loop(0, owned // step, body, 0)

    pack(0)
    pl.semaphore_wait(barrier, n_space - 1 + n_grp - 1)
    halo_start(0)
    labels_start()
    for f in range(1, n_fields):
        pack(f)
        halo_start(f)
    values = make_diagonal()
    for f in range(n_fields):
        stage1(f)
    outer_diagonal(values)
    for t in range(n_fields + 3):
        if t < n_fields:
            stage2(t)
        if 0 <= t - 1 < n_fields:
            stage4(t - 1)
        if 0 <= t - 3 < n_fields:
            stage5(t - 3)

    halo_done(n_fields)
    for f in range(n_fields):
        halo_done(f)
        each(n_space - 1, lambda j: part_copy(f, k, lax.rem(k + 1 + j, n_space)).wait_send())
        each(n_grp - 1, lambda j: a2a_copy(f, g, lax.rem(g + 1 + j, n_grp)).wait_send())
        pltpu.make_async_copy(x.at[f, pl.ds(HALO, planes), inner], out(f), store_sem.at[f]).wait()


def hand_over(a, b, c, out_a, out_b, out_c, held_a, held_b, held_c, sems):
    triples = ((a, held_a, out_a), (b, held_b, out_b), (c, held_c, out_c))
    inward = [pltpu.make_async_copy(i, h, sems.at[0, j]) for j, (i, h, _) in enumerate(triples)]
    outward = [pltpu.make_async_copy(h, o, sems.at[1, j]) for j, (_, h, o) in enumerate(triples)]
    for copy in inward:
        copy.start()
    for first, then in zip(inward, outward):
        first.wait()
        then.start()
    for copy in outward:
        copy.wait()


def solution(mesh):
    n_space, n_grp = mesh.shape["space"], mesh.shape["grp"]

    def local(warm_sources, warm_detectors, source_positions, detector_positions, labels, absorption, residual_codes):
        n_src, planes, breadth, extent = warm_sources.shape
        n_det = warm_detectors.shape[0]
        n = n_src + n_det
        owned = breadth // n_grp
        f32, bf16 = jnp.float32, jnp.bfloat16
        hbm = pl.BlockSpec(memory_space=pl.ANY)
        vmem = pl.BlockSpec(memory_space=pltpu.VMEM)
        sem = pltpu.SemaphoreType.DMA
        tall = (n, planes + 2 * HALO, breadth + 2 * PAD, extent)
        results = pl.pallas_call(
            functools.partial(kernel, n_space, n_grp),
            out_shape=(
                jax.ShapeDtypeStruct(warm_sources.shape, f32),
                jax.ShapeDtypeStruct(warm_detectors.shape, f32),
                jax.ShapeDtypeStruct((planes, owned, extent), f32),
            ),
            in_specs=[hbm] * 7,
            out_specs=(hbm, hbm, vmem),
            scratch_shapes=[
                pltpu.VMEM(tall, f32),
                pltpu.VMEM(tall, f32),
                pltpu.VMEM(tall, f32),
                pltpu.VMEM((planes + 4, breadth, extent), f32),
                pltpu.VMEM((planes, breadth, extent), jnp.int32),
                pltpu.VMEM((n, 2, 2 * breadth + breadth // 2, extent), bf16),
                pltpu.VMEM((n, 2, 2 * breadth + breadth // 2, extent), bf16),
                pltpu.VMEM((2, breadth + breadth // 2, extent), bf16),
                pltpu.VMEM((2, breadth + breadth // 2, extent), bf16),
                pltpu.VMEM((n, n_space, 8, 128), f32),
                pltpu.VMEM((n, planes, breadth, extent), bf16),
                pltpu.VMEM((n, n_grp, planes, owned, extent), bf16),
                pltpu.VMEM((n_grp * n_src, planes, owned, extent), f32),
                pltpu.SMEM(source_positions.shape, jnp.int32),
                pltpu.SMEM(detector_positions.shape, jnp.int32),
                pltpu.SMEM(absorption.shape, f32),
                pltpu.SMEM(residual_codes.shape, jnp.int32),
                sem((4,)),
                sem((n + 1,)),
                sem((n,)),
                sem((n + 1, 2)),
                sem((n + 1, 2)),
                sem((n, n_space)),
                sem((n, n_space)),
                sem((n, n_grp)),
                sem((n, n_grp)),
            ],
            compiler_params=pltpu.CompilerParams(
                collective_id=0, has_side_effects=True, vmem_limit_bytes=60 * 1024 * 1024
            ),
        )(source_positions, detector_positions, absorption, residual_codes, warm_sources, warm_detectors, labels)
        return pl.pallas_call(
            hand_over,
            out_shape=tuple(jax.ShapeDtypeStruct(r.shape, r.dtype) for r in results),
            in_specs=[hbm] * 3,
            out_specs=(hbm,) * 3,
            scratch_shapes=[*(pltpu.VMEM(r.shape, r.dtype) for r in results), sem((2, 3))],
        )(*results)

    fields = P(("recon", "grp"), "space", None, None)
    return jax.shard_map(
        local,
        mesh=mesh,
        in_specs=(
            fields,
            fields,
            P(("recon", "grp")),
            P(("recon", "grp")),
            P(("recon", "space"), None, None),
            P(),
            P("recon", None),
        ),
        out_specs=(fields, fields, P(("recon", "space"), "grp", None)),
        check_vma=False,
    )
```

time: 51.5 us -> 42 us (0.82)
  local copies, waits for them, and re-layouts: 8.73 us -> 0 us
  Pallas kernels: 41.8 us -> 41.1 us
    unnamed x17 -> x0, local copies, waits for them, and re-layouts: 8.73 us -> none
    pallas_call x1, Pallas kernels: 41.8 us -> 38.5 us  [local(): pl.pallas_call(functools.partial(kernel, n_space, n_grp), out_shape=(jax....]
    pallas_call x0 -> x1, Pallas kernels: none -> 2.62 us  [local(): pl.pallas_call(hand_over, out_shape=tuple((jax.ShapeDtypeStruct(r.shape,...]
where the time goes in v2:
time: 42 us; the launch traced here: 41.8 us
  Pallas kernels  41.1 us (98%)
  between operations  0.64 us (2%)
    pallas_call x1, Pallas kernels, local(): pl.pallas_call(functools.partial(kernel, n_space, n_grp), out_shape=(jax....  38.5 us
    pallas_call x1, Pallas kernels, local(): pl.pallas_call(hand_over, out_shape=tuple((jax.ShapeDtypeStruct(r.shape,...  2.62 us

profile of v2, /device:TPU:1, one launch (start us, length us, event | category | flops | bytes accessed | tf_op | source)
XLA Modules:
  0.0 41.8 jit_solution(2342701537622671129)
XLA Ops:
  0.6 38.5 %shard_map.94 = (f32[2,4,128,256]{3,2,1,0:T(8,128)}, f32[2,4,128,256]{3,2,1,0:T(8,128)}, f32[4,32,256]{2,1,0:T(8,128)}) custom-call(s32[2]{0:T(128)} %src_pos_hbm.1, s32[2]{0:T(128)} %det_pos_hbm.1, f32[8]{0:T(128)} %absorption_hbm.1, s32[8,8]{1,0:T(8,128)} %codes_hbm.1, f32[2,4,128,256]{3,2,1,0:T(8,128)} %warm_sources.1, f32[2,4,128,256]{3,2,1,0:T(8,128)} %warm_detectors.1, ...), custom_call_target="tpu_custom_call" | custom-call | tf_op jit(solution)/shard_map/pallas_call | solution.py:464
  39.2 2.6 %shard_map.95 = (f32[2,4,128,256]{3,2,1,0:T(8,128)}, f32[2,4,128,256]{3,2,1,0:T(8,128)}, f32[4,32,256]{2,1,0:T(8,128)}) custom-call(f32[2,4,128,256]{3,2,1,0:T(8,128)} %get-tuple-element.6.a, f32[2,4,128,256]{3,2,1,0:T(8,128)} %get-tuple-element.7.b, f32[4,32,256]{2,1,0:T(8,128)} %get-tuple-element.8.c), custom_call_target="tpu_custom_call" | custom-call | tf_op jit(solution)/shard_map/pallas_call | solution.py:505

commit v3 on v2

--- a/solution.py
+++ b/solution.py
@@ -30,7 +30,7 @@
     x, v0, v1, diag, lab, halo_send, halo_recv, lab_send, lab_recv,
     parts, packed, gathered, mixed,
     src_pos, det_pos, absorption, codes, scalar_sem,
-    load_sem, store_sem, halo_ssem, halo_rsem, part_ssem, part_rsem, a2a_ssem, a2a_rsem,
+    load_sem, store_sem, halo_ssem, halo_rsem, share_ssem, share_rsem, part_ssem, part_rsem, a2a_ssem, a2a_rsem,
 ):
     f32, bf16 = jnp.float32, jnp.bfloat16
     n_src, planes, breadth, extent = warm_sources.shape
@@ -71,34 +71,65 @@
             ((absorption_hbm, absorption), (src_pos_hbm, src_pos), (det_pos_hbm, det_pos), (codes_hbm, codes))
         )
     ]
+    load_labels.start()
     loads[0].start()
     loads[1].start()
-    load_labels.start()
     for copy in scalars:
         copy.start()
     for f in range(2, n_fields):
         loads[f].start()
 
-    border = jnp.zeros((PAD, extent), f32)
-    for f in range(n_fields):
-        for z in range(HALO - 2, HALO + planes + 2):
-            for buf in (x, v0, v1):
-                buf[f, z, pl.ds(0, PAD)] = border
-                buf[f, z, pl.ds(PAD + breadth, PAD)] = border
+    def clear_borders():
+        border = jnp.zeros((PAD, extent), f32)
+        for f in range(n_fields):
+            for z in range(HALO - 2, HALO + planes + 2):
+                for buf in (x, v0, v1):
+                    buf[f, z, pl.ds(0, PAD)] = border
+                    buf[f, z, pl.ds(PAD + breadth, PAD)] = border
 
     def clear(side):
         halo_recv[:, side] = jnp.zeros(halo_recv.shape[:1] + halo_recv.shape[2:], bf16)
         lab_recv[side] = jnp.zeros(lab_recv.shape[1:], bf16)
 
-    pl.when(jnp.logical_not(has_down))(lambda: clear(0))
-    pl.when(jnp.logical_not(has_up))(lambda: clear(1))
     inside = (jnp.where(has_down, 1.0, 0.0), jnp.where(has_up, 1.0, 0.0))
 
+    portion = lab_recv.shape[1] // n_grp
+
+    def share(owner):
+        return pl.ds(pl.multiple_of(owner * portion, 16), portion)
+
+    def share_copy(side, owner, peer):
+        return pltpu.make_async_remote_copy(
+            src_ref=lab_recv.at[side, share(owner)],
+            dst_ref=lab_recv.at[side, share(owner)],
+            send_sem=share_ssem.at[side, peer],
+            recv_sem=share_rsem.at[side, owner],
+            device_id={"grp": peer},
+            device_id_type=MESH,
+        )
+
+    def on_sides(body):
+        pl.when(has_down)(lambda: body(0))
+        pl.when(has_up)(lambda: body(1))
+
+    def share_start(side):
+        halo_copy(n_fields, side == 0).wait_recv()
+        each(n_grp - 1, lambda j: share_copy(side, g, lax.rem(g + 1 + j, n_grp)).start())
+
+    def share_wait(side):
+        each(n_grp - 1, lambda j: share_copy(side, lax.rem(g + 1 + j, n_grp), g).wait_recv())
+
+    def share_done(side):
+        each(n_grp - 1, lambda j: share_copy(side, g, lax.rem(g + 1 + j, n_grp)).wait_send())
+
     def halo_copy(f, up):
-        send, recv = (halo_send.at[f], halo_recv.at[f]) if f < n_fields else (lab_send, lab_recv)
+        if f < n_fields:
+            source, target = halo_send.at[f, 1 if up else 0], halo_recv.at[f, 0 if up else 1]
+        else:
+            source, target = lab_send.at[1 if up else 0, share(g)], lab_recv.at[0 if up else 1, share(g)]
         return pltpu.make_async_remote_copy(
-            src_ref=send.at[1 if up else 0],
-            dst_ref=recv.at[0 if up else 1],
+            src_ref=source,
+            dst_ref=target,
             send_sem=halo_ssem.at[f, 1 if up else 0],
             recv_sem=halo_rsem.at[f, 0 if up else 1],
             device_id={"space": k + 1 if up else k - 1},
@@ -169,7 +200,7 @@
         return value
 
     def outer_diagonal(values):
-        halo_wait(n_fields)
+        on_sides(share_wait)
 
         def body(r, c):
             for side, z in ((0, -1), (1, planes)):
@@ -185,7 +216,7 @@
             return c
         half_loop(half_body, 0)
 
-    def labels_start():
+    def labels_pack():
         load_labels.wait()
 
         def body(r, c):
@@ -201,7 +232,6 @@
             lab_send[1, to] = lab[planes - 2, pl.ds(r, ROWS)].astype(f32).astype(bf16)
             return c
         half_loop(half_body, 0)
-        halo_start(n_fields)
 
     zero = jnp.zeros((8, extent), f32)
     sums = [None] * n_fields
@@ -408,26 +438,35 @@
             return c
         lax.fori_loop(0, owned // step, body, 0)
 
+    labels_pack()
     pack(0)
     pl.semaphore_wait(barrier, n_space - 1 + n_grp - 1)
+    halo_start(n_fields)
     halo_start(0)
-    labels_start()
-    for f in range(1, n_fields):
+    pack(1)
+    halo_start(1)
+    clear_borders()
+    pl.when(jnp.logical_not(has_down))(lambda: clear(0))
+    pl.when(jnp.logical_not(has_up))(lambda: clear(1))
+    for f in range(2, n_fields):
         pack(f)
-        halo_start(f)
     values = make_diagonal()
+    on_sides(share_start)
     for f in range(n_fields):
         stage1(f)
     outer_diagonal(values)
     for t in range(n_fields + 3):
         if t < n_fields:
             stage2(t)
+            if t + 2 < n_fields:
+                halo_start(t + 2)
         if 0 <= t - 1 < n_fields:
             stage4(t - 1)
         if 0 <= t - 3 < n_fields:
             stage5(t - 3)
 
     halo_done(n_fields)
+    on_sides(share_done)
     for f in range(n_fields):
         halo_done(f)
         each(n_space - 1, lambda j: part_copy(f, k, lax.rem(k + 1 + j, n_space)).wait_send())
@@ -493,6 +532,8 @@
                 sem((n,)),
                 sem((n + 1, 2)),
                 sem((n + 1, 2)),
+                sem((2, n_grp)),
+                sem((2, n_grp)),
                 sem((n, n_space)),
                 sem((n, n_space)),
                 sem((n, n_grp)),

time: 42 us -> 38.2 us (0.910)
  Pallas kernels: 41.1 us -> 37.4 us
    pallas_call x1, Pallas kernels: 38.5 us -> 34.7 us  [local(): pl.pallas_call(functools.partial(kernel, n_space, n_grp), out_shape=(jax....]
where the time goes in v3:
time: 38.2 us; the launch traced here: 38 us
  Pallas kernels  37.4 us (98%)
  between operations  0.64 us (2%)
    pallas_call x1, Pallas kernels, local(): pl.pallas_call(functools.partial(kernel, n_space, n_grp), out_shape=(jax....  34.7 us
    pallas_call x1, Pallas kernels, local(): pl.pallas_call(hand_over, out_shape=tuple((jax.ShapeDtypeStruct(r.shape,...  2.62 us

profile of v3, /device:TPU:1, one launch (start us, length us, event | category | flops | bytes accessed | tf_op | source)
XLA Modules:
  0.0 38.0 jit_solution(5765962132038062281)
XLA Ops:
  0.6 34.7 %shard_map.94 = (f32[2,4,128,256]{3,2,1,0:T(8,128)}, f32[2,4,128,256]{3,2,1,0:T(8,128)}, f32[4,32,256]{2,1,0:T(8,128)}) custom-call(s32[2]{0:T(128)} %src_pos_hbm.1, s32[2]{0:T(128)} %det_pos_hbm.1, f32[8]{0:T(128)} %absorption_hbm.1, s32[8,8]{1,0:T(8,128)} %codes_hbm.1, f32[2,4,128,256]{3,2,1,0:T(8,128)} %warm_sources.1, f32[2,4,128,256]{3,2,1,0:T(8,128)} %warm_detectors.1, ...), custom_call_target="tpu_custom_call" | custom-call | tf_op jit(solution)/shard_map/pallas_call | solution.py:503
  35.4 2.6 %shard_map.95 = (f32[2,4,128,256]{3,2,1,0:T(8,128)}, f32[2,4,128,256]{3,2,1,0:T(8,128)}, f32[4,32,256]{2,1,0:T(8,128)}) custom-call(f32[2,4,128,256]{3,2,1,0:T(8,128)} %get-tuple-element.6.a, f32[2,4,128,256]{3,2,1,0:T(8,128)} %get-tuple-element.7.b, f32[4,32,256]{2,1,0:T(8,128)} %get-tuple-element.8.c), custom_call_target="tpu_custom_call" | custom-call | tf_op jit(solution)/shard_map/pallas_call | solution.py:546
